TPU v7x, 32 devices: a whole 2x2x4 slice. The times are simulated.
32 devices in a mesh: dom: 16 (over z, y, core), sub: 2 (over x).
Axes of the slice: x: 2, y: 2, z: 4, core: 2. Of those that a mesh axis runs over, the one named last changes fastest.
Arguments:
- rhs: float32 [2, 24576], P(None, ('dom', 'sub')), may hold values from -6 to 6
- start: float32 [2, 24576], P(None, ('dom', 'sub')), may hold values from -6 to 6
- stiffness: bfloat16 [24576, 768], P(('dom', 'sub')), may hold values from -0.109375 to 0.109375
- local_inverse: bfloat16 [24576, 768], P(('dom', 'sub')), may hold values from -0.109375 to 0.109375
- basis: bfloat16 [24, 24576], P(None, ('dom', 'sub')), may hold values from -0.21875 to 0.21875
- weights: float32 [24576], P(('dom', 'sub')), may hold values from 0.3 to 1
- coarse_inverse: float32 [768, 768], P(('dom', 'sub')), may hold values from -0.4375 to 0.4375
- orders: int32 [32], P(('dom', 'sub')), may hold values from 192 to 768, as said below
- out_rows: int32 [32, 6, 128], P(('dom', 'sub')), may hold values from 0 to 191
- out_counts: int32 [32, 6], P(('dom', 'sub')), may hold values from 0 to 128, as said below
- in_rows: int32 [32, 6, 128], P(('dom', 'sub')), may hold values from 0 to 191
Outputs:
- solution: float32 [2, 24576], P(None, ('dom', 'sub'))
- residual: float32 [2, 24576], P(None, ('dom', 'sub'))
Inputs may be any that keep to these rules, and one draw needn't show every extreme that they name: `orders`: some subdomain has order exactly 768, another exactly 192. `out_rows`: every listed row lies below every subdomain's order. `in_rows`: every listed row lies below every subdomain's order. `out_counts`: some direction of some subdomain uses all 128 slots.
All inputs are finite; a program needn't handle non-finite values.
Results may differ from a plain program's by a relative error of at most 0.0019.
Values sent between devices are 32-bit elements; how exact they have to be, the bound alone decides.
A program may use at most 64 MiB of HBM per device.

v0:
```python
import jax
import jax.numpy as jnp
from jax import lax
from jax.sharding import PartitionSpec as P

DIRECTIONS = (("sub", 1), ("sub", -1), ("dom", 1), ("dom", -1), ("dom", 2), ("dom", -2))


def passed_along(block, axis, distance):
    devices = range(lax.axis_size(axis))
    route = [(i - distance, i) for i in devices if i - distance in devices]
    return lax.ppermute(block, axis, route)


def assemble(terms, out_rows, out_counts, in_rows):
    slot_ids = jnp.arange(out_rows.shape[2])
    summed = terms
    for index_dir, (axis_name, offset) in enumerate(DIRECTIONS):
        used = (slot_ids < out_counts[0, index_dir]).astype(jnp.float32)
        picked = terms[:, out_rows[0, index_dir]] * used[None, :]
        if axis_name == "sub":
            arrived = passed_along(picked, "sub", offset)
        else:
            arrived = passed_along(picked, "dom", offset)
        summed = summed.at[:, in_rows[0, index_dir]].add(arrived)
    return summed


def per_device(
    rhs,
    start,
    stiffness,
    local_inverse,
    basis,
    weights,
    coarse_inverse,
    orders,
    out_rows,
    out_counts,
    in_rows,
):
    order_pad = stiffness.shape[0]
    row_mask = (jnp.arange(order_pad) < orders[0]).astype(jnp.float32)[None, :]
    iterate = start * row_mask
    weight_rows = weights[None, :]
    iterate_bf = iterate.astype(jnp.bfloat16)
    product = jnp.dot(iterate_bf, stiffness, preferred_element_type=jnp.float32)
    residual = row_mask * (rhs - assemble(product, out_rows, out_counts, in_rows))
    residual_bf = residual.astype(jnp.bfloat16)
    coarse_in = lax.dot_general(
        residual_bf, basis, (((1,), (1,)), ((), ())), preferred_element_type=jnp.float32
    )
    grouped = lax.all_gather(coarse_in, "sub", axis=1, tiled=True)
    coarse_out = lax.dot_general(
        lax.all_gather(grouped, "dom", axis=1, tiled=True),
        coarse_inverse,
        (((1,), (1,)), ((), ())),
        precision=lax.Precision.HIGHEST,
        preferred_element_type=jnp.float32,
    )
    local_fix = jnp.dot(residual_bf, local_inverse, preferred_element_type=jnp.float32)
    coarse_fix = jnp.dot(coarse_out.astype(jnp.bfloat16), basis, preferred_element_type=jnp.float32)
    correction = weight_rows * row_mask * (local_fix + coarse_fix)
    iterate = iterate + assemble(correction, out_rows, out_counts, in_rows)
    return (iterate, residual)


def solution(mesh):
    return jax.shard_map(
        per_device,
        mesh=mesh,
        in_specs=(
            P(None, ("dom", "sub")),
            P(None, ("dom", "sub")),
            P(("dom", "sub"), None),
            P(("dom", "sub"), None),
            P(None, ("dom", "sub")),
            P(("dom", "sub")),
            P(("dom", "sub"), None),
            P(("dom", "sub")),
            P(("dom", "sub"), None, None),
            P(("dom", "sub"), None),
            P(("dom", "sub"), None, None),
        ),
        out_specs=(P(None, ("dom", "sub")), P(None, ("dom", "sub"))),
        check_vma=False,
    )
```

profile of v0, /device:TPU:0, one launch (start us, length us, event | category | flops | bytes accessed | tf_op | source)
XLA Modules:
  0.0 94.6 jit_solution(3323255881209918410)
XLA Ops:
  1.4 0.7 fusion.43
  2.1 1.5 %fusion.44 = (s32[1,1]{1,0:T(1,128)}, s32[1,1]{1,0:T(1,128)}, s32[1,1]{1,0:T(1,128)}, s32[1,1]{1,0:T(1,128)}, s32[1,1]{1,0:T(1,128)}, /*index=5*/s32[1,1]{1,0:T(1,128)}) fusion(s32[1,6]{1,0:T(1,128)} %param.20), kind=kLoop, calls=%fused_computation.111 | loop fusion | bytes 48 | tf_op jit(solution)/shard_map/slice | solution.py:19
  4.4 1.3 %fusion.27 = f32[2,768]{0,1:T(8,128)S(1)} fusion(bf16[768,768]{1,0:T(8,128)(2,1)S(1)} %copy-done, f32[2,768]{1,0:T(2,128)} %param.12, f32[768]{0:T(1024)S(1)} %fusion.26), kind=kOutput, calls=%fused_computation.76 | convolution fusion | flops 2362368 | bytes 1195008 | tf_op jit(solution)/shard_map/dot_general | solution.py:47
  6.4 1.3 %collective-permute-start.5 = (f32[2,128]{0,1:T(8,128)S(1)}, f32[2,128]{0,1:T(8,128)S(1)}, u32[]{:S(2)}, u32[]{:S(2)}) collective-permute-start(f32[2,128]{0,1:T(8,128)S(1)} %multiply_bitcast_fusion.6), channel_id=1, source_target_pairs={{4,0},{6,2},{8,4},{10,6},{12,8},{14,10},{16,12},{18,14},{20,16},{2... | collective-permute-start | bytes 3080 | tf_op jit(solution)/shard_map/ppermute | solution.py:12
  9.1 4.8 %collective-permute-start = (f32[2,128]{0,1:T(8,128)S(1)}, f32[2,128]{0,1:T(8,128)S(1)}, u32[]{:S(2)}, u32[]{:S(2)}) collective-permute-start(f32[2,128]{0,1:T(8,128)S(1)} %multiply_bitcast_fusion.11), channel_id=1, source_target_pairs={{0,1},{2,3},{4,5},{6,7},{8,9},{10,11},{12,13},{14,15},{16,17},{18,... | collective-permute-start | bytes 3080 | tf_op jit(solution)/shard_map/ppermute | solution.py:12
  15.3 1.3 %collective-permute-start.1 = (f32[2,128]{0,1:T(8,128)S(1)}, f32[2,128]{0,1:T(8,128)S(1)}, u32[]{:S(2)}, u32[]{:S(2)}) collective-permute-start(f32[2,128]{0,1:T(8,128)S(1)} %multiply_bitcast_fusion.10), channel_id=1, source_target_pairs={{1,0},{3,2},{5,4},{7,6},{9,8},{11,10},{13,12},{15,14},{17,16},{19,... | collective-permute-start | bytes 3080 | tf_op jit(solution)/shard_map/ppermute | solution.py:12
  17.9 1.5 %collective-permute-start.2 = (f32[2,128]{0,1:T(8,128)S(1)}, f32[2,128]{0,1:T(8,128)S(1)}, u32[]{:S(2)}, u32[]{:S(2)}) collective-permute-start(f32[2,128]{0,1:T(8,128)S(1)} %multiply_bitcast_fusion.9), channel_id=1, source_target_pairs={{0,2},{2,4},{4,6},{6,8},{8,10},{10,12},{12,14},{14,16},{16,18},{18... | collective-permute-start | bytes 3080 | tf_op jit(solution)/shard_map/ppermute | solution.py:12
  19.4 0.7 compare_convert_fusion.2
  20.8 1.3 %collective-permute-start.3 = (f32[2,128]{0,1:T(8,128)S(1)}, f32[2,128]{0,1:T(8,128)S(1)}, u32[]{:S(2)}, u32[]{:S(2)}) collective-permute-start(f32[2,128]{0,1:T(8,128)S(1)} %multiply_bitcast_fusion.8), channel_id=1, source_target_pairs={{2,0},{4,2},{6,4},{8,6},{10,8},{12,10},{14,12},{16,14},{18,16},{20... | collective-permute-start | bytes 3080 | tf_op jit(solution)/shard_map/ppermute | solution.py:12
  23.5 7.4 %collective-permute-start.4 = (f32[2,128]{0,1:T(8,128)S(1)}, f32[2,128]{0,1:T(8,128)S(1)}, u32[]{:S(2)}, u32[]{:S(2)}) collective-permute-start(f32[2,128]{0,1:T(8,128)S(1)} %multiply_bitcast_fusion.7), channel_id=1, source_target_pairs={{0,4},{2,6},{4,8},{6,10},{8,12},{10,14},{12,16},{14,18},{16,20},{1... | collective-permute-start | bytes 3080 | tf_op jit(solution)/shard_map/ppermute | solution.py:12
  30.9 1.4 %scatter_custom_fusion = f32[2,768]{0,1:T(8,128)S(1)} fusion(f32[2,768]{0,1:T(8,128)S(1)} %fusion.27, s32[128]{0:T(128)S(1)} %get-tuple-element.18, f32[2,128]{0,1:T(8,128)S(1)} %collective-permute-done), kind=kCustom, calls=%fused_computation.50 | custom fusion | flops 256 | bytes 71680 | tf_op jit(solution)/shard_map/scatter-add | solution.py:25
  32.4 1.4 %scatter_custom_fusion.1 = f32[2,768]{0,1:T(8,128)S(1)} fusion(f32[2,768]{0,1:T(8,128)S(1)} %scatter_custom_fusion, s32[128]{0:T(128)S(1)} %get-tuple-element.17, f32[2,128]{0,1:T(8,128)S(1)} %collective-permute-done.1), kind=kCustom, calls=%fused_computation.48 | custom fusion | flops 256 | bytes 71680 | tf_op jit(solution)/shard_map/scatter-add | solution.py:25
  33.8 1.4 %scatter_custom_fusion.2 = f32[2,768]{0,1:T(8,128)S(1)} fusion(f32[2,768]{0,1:T(8,128)S(1)} %scatter_custom_fusion.1, s32[128]{0:T(128)S(1)} %get-tuple-element.16, f32[2,128]{0,1:T(8,128)S(1)} %collective-permute-done.2), kind=kCustom, calls=%fused_computation.46 | custom fusion | flops 256 | bytes 71680 | tf_op jit(solution)/shard_map/scatter-add | solution.py:25
  35.3 1.4 %scatter_custom_fusion.3 = f32[2,768]{0,1:T(8,128)S(1)} fusion(f32[2,768]{0,1:T(8,128)S(1)} %scatter_custom_fusion.2, s32[128]{0:T(128)S(1)} %get-tuple-element.15, f32[2,128]{0,1:T(8,128)S(1)} %collective-permute-done.3), kind=kCustom, calls=%fused_computation.44 | custom fusion | flops 256 | bytes 71680 | tf_op jit(solution)/shard_map/scatter-add | solution.py:25
  36.7 1.4 %scatter_custom_fusion.4 = f32[2,768]{0,1:T(8,128)S(1)} fusion(f32[2,768]{0,1:T(8,128)S(1)} %scatter_custom_fusion.3, s32[128]{0:T(128)S(1)} %get-tuple-element.19, f32[2,128]{0,1:T(8,128)S(1)} %collective-permute-done.4), kind=kCustom, calls=%fused_computation.42 | custom fusion | flops 256 | bytes 71680 | tf_op jit(solution)/shard_map/scatter-add | solution.py:25
  38.2 1.4 %scatter_custom_fusion.5 = f32[2,768]{0,1:T(8,128)S(1)} fusion(f32[2,768]{0,1:T(8,128)S(1)} %scatter_custom_fusion.4, s32[128]{0:T(128)S(1)} %get-tuple-element.14, f32[2,128]{0,1:T(8,128)S(1)} %collective-permute-done.5), kind=kCustom, calls=%fused_computation.40 | custom fusion | flops 256 | bytes 71680 | tf_op jit(solution)/shard_map/scatter-add | solution.py:25
  39.9 4.8 %all-gather = f32[2,24,2]{1,2,0:T(2,128)S(1)} all-gather(f32[1,24,2]{1,2,0:T(2,128)S(1)} %convolution_bitcast_fusion), channel_id=1, replica_groups=mesh['dom'=16,'sub'=2] {'sub'}, dimensions={0}, use_global_device_ids=true | all-gather | bytes 576 | tf_op jit(solution)/shard_map/all_gather | solution.py:53
  45.1 20.6 %all-gather.1 = f32[16,48,2]{1,2,0:T(2,128)S(1)} all-gather(f32[1,48,2]{1,2,0:T(2,128)S(1)} %reshape.571), channel_id=1, replica_groups=mesh['dom'=16,'sub'=2] {'dom'}, dimensions={0}, use_global_device_ids=true | all-gather | bytes 6528 | tf_op jit(solution)/shard_map/all_gather | solution.py:55
  66.4 0.7 gather_fusion.11
  70.7 1.3 %collective-permute-start.7 = (f32[2,128]{0,1:T(8,128)S(1)}, f32[2,128]{0,1:T(8,128)S(1)}, u32[]{:S(2)}, u32[]{:S(2)}) collective-permute-start(f32[2,128]{0,1:T(8,128)S(1)} %multiply_bitcast_fusion.4), channel_id=1, source_target_pairs={{1,0},{3,2},{5,4},{7,6},{9,8},{11,10},{13,12},{15,14},{17,16},{19,... | collective-permute-start | bytes 3080 | tf_op jit(solution)/shard_map/ppermute | solution.py:12
  72.0 4.5 %collective-permute-start.6 = (f32[2,128]{0,1:T(8,128)S(1)}, f32[2,128]{0,1:T(8,128)S(1)}, u32[]{:S(2)}, u32[]{:S(2)}) collective-permute-start(f32[2,128]{0,1:T(8,128)S(1)} %multiply_bitcast_fusion.5), channel_id=1, source_target_pairs={{0,1},{2,3},{4,5},{6,7},{8,9},{10,11},{12,13},{14,15},{16,17},{18,... | collective-permute-start | bytes 3080 | tf_op jit(solution)/shard_map/ppermute | solution.py:12
  76.5 1.7 %collective-permute-start.8 = (f32[2,128]{0,1:T(8,128)S(1)}, f32[2,128]{0,1:T(8,128)S(1)}, u32[]{:S(2)}, u32[]{:S(2)}) collective-permute-start(f32[2,128]{0,1:T(8,128)S(1)} %multiply_bitcast_fusion.3), channel_id=1, source_target_pairs={{0,2},{2,4},{4,6},{6,8},{8,10},{10,12},{12,14},{14,16},{16,18},{18... | collective-permute-start | bytes 3080 | tf_op jit(solution)/shard_map/ppermute | solution.py:12
  78.2 1.3 %collective-permute-start.9 = (f32[2,128]{0,1:T(8,128)S(1)}, f32[2,128]{0,1:T(8,128)S(1)}, u32[]{:S(2)}, u32[]{:S(2)}) collective-permute-start(f32[2,128]{0,1:T(8,128)S(1)} %multiply_bitcast_fusion.2), channel_id=1, source_target_pairs={{2,0},{4,2},{6,4},{8,6},{10,8},{12,10},{14,12},{16,14},{18,16},{20... | collective-permute-start | bytes 3080 | tf_op jit(solution)/shard_map/ppermute | solution.py:12
  79.6 4.2 %collective-permute-start.10 = (f32[2,128]{0,1:T(8,128)S(1)}, f32[2,128]{0,1:T(8,128)S(1)}, u32[]{:S(2)}, u32[]{:S(2)}) collective-permute-start(f32[2,128]{0,1:T(8,128)S(1)} %multiply_bitcast_fusion.1), channel_id=1, source_target_pairs={{0,4},{2,6},{4,8},{6,10},{8,12},{10,14},{12,16},{14,18},{16,20},{1... | collective-permute-start | bytes 3080 | tf_op jit(solution)/shard_map/ppermute | solution.py:12
  83.8 1.3 %collective-permute-start.11 = (f32[2,128]{0,1:T(8,128)S(1)}, f32[2,128]{0,1:T(8,128)S(1)}, u32[]{:S(2)}, u32[]{:S(2)}) collective-permute-start(f32[2,128]{0,1:T(8,128)S(1)} %multiply_bitcast_fusion), channel_id=1, source_target_pairs={{4,0},{6,2},{8,4},{10,6},{12,8},{14,10},{16,12},{18,14},{20,16},{2... | collective-permute-start | bytes 3080 | tf_op jit(solution)/shard_map/ppermute | solution.py:12
  85.3 1.4 %scatter_custom_fusion.6 = f32[2,768]{0,1:T(8,128)S(1)} fusion(f32[2,768]{0,1:T(8,128)S(1)} %copy.59, s32[128]{0:T(128)S(1)} %get-tuple-element.18, f32[2,128]{0,1:T(8,128)S(1)} %collective-permute-done.6), kind=kCustom, calls=%fused_computation.38 | custom fusion | flops 256 | bytes 71680 | tf_op jit(solution)/shard_map/scatter-add | solution.py:25
  86.7 1.4 %scatter_custom_fusion.7 = f32[2,768]{0,1:T(8,128)S(1)} fusion(f32[2,768]{0,1:T(8,128)S(1)} %scatter_custom_fusion.6, s32[128]{0:T(128)S(1)} %get-tuple-element.17, f32[2,128]{0,1:T(8,128)S(1)} %collective-permute-done.7), kind=kCustom, calls=%fused_computation.36 | custom fusion | flops 256 | bytes 71680 | tf_op jit(solution)/shard_map/scatter-add | solution.py:25
  88.1 1.4 %scatter_custom_fusion.8 = f32[2,768]{0,1:T(8,128)S(1)} fusion(f32[2,768]{0,1:T(8,128)S(1)} %scatter_custom_fusion.7, s32[128]{0:T(128)S(1)} %get-tuple-element.16, f32[2,128]{0,1:T(8,128)S(1)} %collective-permute-done.8), kind=kCustom, calls=%fused_computation.34 | custom fusion | flops 256 | bytes 71680 | tf_op jit(solution)/shard_map/scatter-add | solution.py:25
  89.6 1.4 %scatter_custom_fusion.9 = f32[2,768]{0,1:T(8,128)S(1)} fusion(f32[2,768]{0,1:T(8,128)S(1)} %scatter_custom_fusion.8, s32[128]{0:T(128)S(1)} %get-tuple-element.15, f32[2,128]{0,1:T(8,128)S(1)} %collective-permute-done.9), kind=kCustom, calls=%fused_computation.32 | custom fusion | flops 256 | bytes 71680 | tf_op jit(solution)/shard_map/scatter-add | solution.py:25
  91.0 1.4 %scatter_custom_fusion.10 = f32[2,768]{0,1:T(8,128)S(1)} fusion(f32[2,768]{0,1:T(8,128)S(1)} %scatter_custom_fusion.9, s32[128]{0:T(128)S(1)} %get-tuple-element.19, f32[2,128]{0,1:T(8,128)S(1)} %collective-permute-done.10), kind=kCustom, calls=%fused_computation.30 | custom fusion | flops 256 | bytes 71680 | tf_op jit(solution)/shard_map/scatter-add | solution.py:25
  92.4 1.4 %scatter_custom_fusion.11 = f32[2,768]{0,1:T(8,128)S(1)} fusion(f32[2,768]{0,1:T(8,128)S(1)} %scatter_custom_fusion.10, s32[128]{0:T(128)S(1)} %get-tuple-element.14, f32[2,128]{0,1:T(8,128)S(1)} %collective-permute-done.11), kind=kCustom, calls=%fused_computation.28 | custom fusion | flops 256 | bytes 71680 | tf_op jit(solution)/shard_map/scatter-add | solution.py:25
  93.9 0.7 copy.65
  (76 shorter events, 12.7 us)
Async XLA Ops:
  0.6 3.7 %copy-start = (bf16[768,768]{1,0:T(8,128)(2,1)S(1)}, bf16[768,768]{1,0:T(8,128)(2,1)}, u32[]{:S(2)}) copy-start(bf16[768,768]{1,0:T(8,128)(2,1)} %param.13) | copy-start | bytes 3538948
  4.4 19.1 %copy-start.7 = (f32[768]{0:T(1024)S(1)}, f32[768]{0:T(1024)}, u32[]{:S(2)}) copy-start(f32[768]{0:T(1024)} %param.16) | copy-start | bytes 9220
  4.4 26.5 %copy-start.8 = (s32[1,6,128]{2,0,1:T(1,128)S(1)}, s32[1,6,128]{2,0,1:T(1,128)}, u32[]{:S(2)}) copy-start(s32[1,6,128]{2,0,1:T(1,128)} %param.21) | copy-start | bytes 9220
  6.4 31.7 %collective-permute-start.5 = (f32[2,128]{0,1:T(8,128)S(1)}, f32[2,128]{0,1:T(8,128)S(1)}, u32[]{:S(2)}, u32[]{:S(2)}) collective-permute-start(f32[2,128]{0,1:T(8,128)S(1)} %multiply_bitcast_fusion.6), channel_id=1, source_target_pairs={{4,0},{6,2},{8,4},{10,6},{12,8},{14,10},{16,12},{18,14},{20,16},{2... | collective-permute-start | bytes 3080 | tf_op jit(solution)/shard_map/ppermute | solution.py:12
  9.1 14.4 %collective-permute-start = (f32[2,128]{0,1:T(8,128)S(1)}, f32[2,128]{0,1:T(8,128)S(1)}, u32[]{:S(2)}, u32[]{:S(2)}) collective-permute-start(f32[2,128]{0,1:T(8,128)S(1)} %multiply_bitcast_fusion.11), channel_id=1, source_target_pairs={{0,1},{2,3},{4,5},{6,7},{8,9},{10,11},{12,13},{14,15},{16,17},{18,... | collective-permute-start | bytes 3080 | tf_op jit(solution)/shard_map/ppermute | solution.py:12
  15.3 17.0 %collective-permute-start.1 = (f32[2,128]{0,1:T(8,128)S(1)}, f32[2,128]{0,1:T(8,128)S(1)}, u32[]{:S(2)}, u32[]{:S(2)}) collective-permute-start(f32[2,128]{0,1:T(8,128)S(1)} %multiply_bitcast_fusion.10), channel_id=1, source_target_pairs={{1,0},{3,2},{5,4},{7,6},{9,8},{11,10},{13,12},{15,14},{17,16},{19,... | collective-permute-start | bytes 3080 | tf_op jit(solution)/shard_map/ppermute | solution.py:12
  17.9 15.9 %collective-permute-start.2 = (f32[2,128]{0,1:T(8,128)S(1)}, f32[2,128]{0,1:T(8,128)S(1)}, u32[]{:S(2)}, u32[]{:S(2)}) collective-permute-start(f32[2,128]{0,1:T(8,128)S(1)} %multiply_bitcast_fusion.9), channel_id=1, source_target_pairs={{0,2},{2,4},{4,6},{6,8},{8,10},{10,12},{12,14},{14,16},{16,18},{18... | collective-permute-start | bytes 3080 | tf_op jit(solution)/shard_map/ppermute | solution.py:12
  20.8 14.4 %collective-permute-start.3 = (f32[2,128]{0,1:T(8,128)S(1)}, f32[2,128]{0,1:T(8,128)S(1)}, u32[]{:S(2)}, u32[]{:S(2)}) collective-permute-start(f32[2,128]{0,1:T(8,128)S(1)} %multiply_bitcast_fusion.8), channel_id=1, source_target_pairs={{2,0},{4,2},{6,4},{8,6},{10,8},{12,10},{14,12},{16,14},{18,16},{20... | collective-permute-start | bytes 3080 | tf_op jit(solution)/shard_map/ppermute | solution.py:12
  23.5 13.2 %collective-permute-start.4 = (f32[2,128]{0,1:T(8,128)S(1)}, f32[2,128]{0,1:T(8,128)S(1)}, u32[]{:S(2)}, u32[]{:S(2)}) collective-permute-start(f32[2,128]{0,1:T(8,128)S(1)} %multiply_bitcast_fusion.7), channel_id=1, source_target_pairs={{0,4},{2,6},{4,8},{6,10},{8,12},{10,14},{12,16},{14,18},{16,20},{1... | collective-permute-start | bytes 3080 | tf_op jit(solution)/shard_map/ppermute | solution.py:12
  33.8 6.0 %copy-start.6 = (f32[2,768]{1,0:T(2,128)S(1)}, f32[2,768]{1,0:T(2,128)}, u32[]{:S(2)}) copy-start(f32[2,768]{1,0:T(2,128)} %param.11) | copy-start | bytes 18436
  33.8 6.0 %copy-start.3 = (bf16[24,768]{1,0:T(8,128)(2,1)S(1)}, bf16[24,768]{1,0:T(8,128)(2,1)}, u32[]{:S(2)}) copy-start(bf16[24,768]{1,0:T(8,128)(2,1)} %param.15) | copy-start | bytes 110596
  33.8 11.0 %copy-start.1 = (bf16[768,768]{1,0:T(8,128)(2,1)S(1)}, bf16[768,768]{1,0:T(8,128)(2,1)}, u32[]{:S(2)}) copy-start(bf16[768,768]{1,0:T(8,128)(2,1)} %param.14) | copy-start | bytes 3538948
  38.1 27.7 %copy-start.2 = (f32[24,768]{1,0:T(8,128)S(1)}, f32[24,768]{1,0:T(8,128)}, u32[]{:S(2)}) copy-start(f32[24,768]{1,0:T(8,128)} %param.17) | copy-start | bytes 221188
  38.1 27.9 %copy-start.4 = (f32[2,768]{1,0:T(2,128)S(1)}, f32[2,768]{1,0:T(2,128)}, u32[]{:S(2)}) copy-start(f32[2,768]{1,0:T(2,128)} %param.12) | copy-start | bytes 18436
  39.8 30.8 %copy-start.5 = (f32[2,768]{1,0:T(2,128)}, f32[2,768]{1,0:T(2,128)S(1)}, u32[]{:S(2)}) copy-start(f32[2,768]{1,0:T(2,128)S(1)} %subtract_multiply_fusion) | copy-start | bytes 18436
  70.7 16.0 %collective-permute-start.7 = (f32[2,128]{0,1:T(8,128)S(1)}, f32[2,128]{0,1:T(8,128)S(1)}, u32[]{:S(2)}, u32[]{:S(2)}) collective-permute-start(f32[2,128]{0,1:T(8,128)S(1)} %multiply_bitcast_fusion.4), channel_id=1, source_target_pairs={{1,0},{3,2},{5,4},{7,6},{9,8},{11,10},{13,12},{15,14},{17,16},{19,... | collective-permute-start | bytes 3080 | tf_op jit(solution)/shard_map/ppermute | solution.py:12
  72.0 11.8 %collective-permute-start.6 = (f32[2,128]{0,1:T(8,128)S(1)}, f32[2,128]{0,1:T(8,128)S(1)}, u32[]{:S(2)}, u32[]{:S(2)}) collective-permute-start(f32[2,128]{0,1:T(8,128)S(1)} %multiply_bitcast_fusion.5), channel_id=1, source_target_pairs={{0,1},{2,3},{4,5},{6,7},{8,9},{10,11},{12,13},{14,15},{16,17},{18,... | collective-permute-start | bytes 3080 | tf_op jit(solution)/shard_map/ppermute | solution.py:12
  76.5 11.6 %collective-permute-start.8 = (f32[2,128]{0,1:T(8,128)S(1)}, f32[2,128]{0,1:T(8,128)S(1)}, u32[]{:S(2)}, u32[]{:S(2)}) collective-permute-start(f32[2,128]{0,1:T(8,128)S(1)} %multiply_bitcast_fusion.3), channel_id=1, source_target_pairs={{0,2},{2,4},{4,6},{6,8},{8,10},{10,12},{12,14},{14,16},{16,18},{18... | collective-permute-start | bytes 3080 | tf_op jit(solution)/shard_map/ppermute | solution.py:12
  78.2 11.4 %collective-permute-start.9 = (f32[2,128]{0,1:T(8,128)S(1)}, f32[2,128]{0,1:T(8,128)S(1)}, u32[]{:S(2)}, u32[]{:S(2)}) collective-permute-start(f32[2,128]{0,1:T(8,128)S(1)} %multiply_bitcast_fusion.2), channel_id=1, source_target_pairs={{2,0},{4,2},{6,4},{8,6},{10,8},{12,10},{14,12},{16,14},{18,16},{20... | collective-permute-start | bytes 3080 | tf_op jit(solution)/shard_map/ppermute | solution.py:12
  79.6 11.4 %collective-permute-start.10 = (f32[2,128]{0,1:T(8,128)S(1)}, f32[2,128]{0,1:T(8,128)S(1)}, u32[]{:S(2)}, u32[]{:S(2)}) collective-permute-start(f32[2,128]{0,1:T(8,128)S(1)} %multiply_bitcast_fusion.1), channel_id=1, source_target_pairs={{0,4},{2,6},{4,8},{6,10},{8,12},{10,14},{12,16},{14,18},{16,20},{1... | collective-permute-start | bytes 3080 | tf_op jit(solution)/shard_map/ppermute | solution.py:12
  83.8 8.7 %collective-permute-start.11 = (f32[2,128]{0,1:T(8,128)S(1)}, f32[2,128]{0,1:T(8,128)S(1)}, u32[]{:S(2)}, u32[]{:S(2)}) collective-permute-start(f32[2,128]{0,1:T(8,128)S(1)} %multiply_bitcast_fusion), channel_id=1, source_target_pairs={{4,0},{6,2},{8,4},{10,6},{12,8},{14,10},{16,12},{18,14},{20,16},{2... | collective-permute-start | bytes 3080 | tf_op jit(solution)/shard_map/ppermute | solution.py:12
where the time goes:
time: 95.7 us; the launch traced here: 94.6 us
  starting transfers between devices  31.8 us (33%)
  blocking collectives  25.5 us (27%)
  other arithmetic  22.5 us (24%)
  local copies, waits for them, and re-layouts  10.8 us (11%)
  between operations  2.01 us (2%)
  matrix products  1.99 us (2%)
    ppermute x12, starting transfers between devices, passed_along(): return lax.ppermute(block, axis, route)  31.8 us
    all_gather x1, blocking collectives, per_device(): lax.all_gather(grouped, 'dom', axis=1, tiled=True)  20.6 us
    scatter-add x12, other arithmetic, assemble(): summed = summed.at[:, in_rows[0, index_dir]].add(arrived)  17 us
    gather x12, local copies, waits for them, and re-layouts, assemble(): picked = terms[:, out_rows[0, index_dir]] * used[None, :]  7.75 us
    all_gather x1, blocking collectives, per_device(): grouped = lax.all_gather(coarse_in, 'sub', axis=1, tiled=True)  4.84 us
    convert_element_type x6, other arithmetic, assemble(): used = (slot_ids < out_counts[0, index_dir]).astype(jnp.float32)  3.78 us
  transfers between devices with their start and end apart: 12, of which 0 were waited for; matrix products, arithmetic and copies ran while one was open for 22% of the time, Pallas kernels for 0%

commit v1 on v0

v1 whole, which is shorter than its diff:
```python
import functools
import math

import jax
import jax.numpy as jnp
from jax import lax
from jax.experimental import pallas as pl
from jax.experimental.pallas import tpu as pltpu
from jax.sharding import PartitionSpec as P

DIRECTIONS = (("sub", 1), ("sub", -1), ("dom", 1), ("dom", -1), ("dom", 2), ("dom", -2))
MESH = pl.DeviceIdType.MESH
LANES = 128


def halves(x):
    high = x.astype(jnp.bfloat16).astype(jnp.float32)
    return jnp.concatenate([high, x - high], axis=0).astype(jnp.bfloat16)


def dot(a, b):
    return jnp.dot(a, b, preferred_element_type=jnp.float32)


def dot_t(a, b):
    return lax.dot_general(a, b, (((1,), (1,)), ((), ())), preferred_element_type=jnp.float32)


def exact_dot(x, picker, by=dot):
    rows = x.shape[0]
    both = by(halves(x), picker)
    return both[:rows] + both[rows:]


def kernel(
    n_dom,
    n_sub,
    rhs_hbm,
    start_hbm,
    stiff_hbm,
    inverse_hbm,
    basis_hbm,
    weights_hbm,
    coarse_hbm,
    orders_hbm,
    out_rows_hbm,
    out_counts_hbm,
    in_rows_hbm,
    solution_hbm,
    residual_hbm,
    rhs,
    start,
    stiff,
    inverse,
    basis,
    weights,
    coarse,
    orders,
    out_rows,
    out_counts,
    in_rows,
    picker,
    placer,
    basis_pad,
    coarse_pad,
    sent_first,
    sent_second,
    came_first,
    came_second,
    gathered,
    solution_out,
    residual_out,
    load_sems,
    store_sems,
    send_first,
    recv_first,
    send_second,
    recv_second,
    gather_send,
    gather_recv,
):
    devices = n_dom * n_sub
    loads, order_pad = rhs.shape
    slots = out_rows.shape[1]
    vectors = basis.shape[0]
    head = placer.shape[0]
    dom, sub = lax.axis_index("dom"), lax.axis_index("sub")
    me = dom * n_sub + sub

    def load(index, source, target):
        copy = pltpu.make_async_copy(source, target, load_sems.at[index])
        copy.start()
        return copy

    got_start = load(0, start_hbm, start)
    got_orders = load(1, orders_hbm, orders)
    got_head = load(2, stiff_hbm.at[:, :head], stiff.at[:, :head])
    got_out = load(3, out_rows_hbm, out_rows)
    got_counts = load(4, out_counts_hbm, out_counts)
    got_tail = load(5, stiff_hbm.at[:, head:], stiff.at[:, head:])
    got_in = load(6, in_rows_hbm, in_rows)
    got_rhs = load(7, rhs_hbm, rhs)
    got_basis = load(8, basis_hbm, basis)
    got_weights = load(9, weights_hbm, weights)
    got_inverse = load(10, inverse_hbm, inverse)
    got_coarse = load(11, coarse_hbm, coarse)

    came_first[...] = jnp.zeros_like(came_first)
    came_second[...] = jnp.zeros_like(came_second)

    barrier = pltpu.get_barrier_semaphore()

    def device_of(step):
        peer = lax.rem(me + step, devices)
        return (lax.div(peer, n_sub), lax.rem(peer, n_sub))

    def greet(step, carry):
        pl.semaphore_signal(barrier, inc=1, device_id=device_of(step), device_id_type=MESH)
        return carry

    lax.fori_loop(1, devices, greet, 0)

    def exchange(sent, came, send_sems, recv_sems):
        moves = []
        for index_dir, (axis_name, offset) in enumerate(DIRECTIONS):
            here, length = (sub, n_sub) if axis_name == "sub" else (dom, n_dom)
            there = here + offset
            target = (dom, there) if axis_name == "sub" else (there, sub)
            sends = (there >= 0) & (there < length)
            receives = (here - offset >= 0) & (here - offset < length)
            copy = pltpu.make_async_remote_copy(
                src_ref=sent.at[index_dir],
                dst_ref=came.at[index_dir],
                send_sem=send_sems.at[index_dir],
                recv_sem=recv_sems.at[index_dir],
                device_id=target,
                device_id_type=MESH,
            )
            pl.when(sends)(copy.start)
            moves.append((copy, sends, receives))
        return moves

    def wait_arrivals(moves):
        for copy, _, receives in moves:
            pl.when(receives)(copy.wait_recv)

    def arrived_rows(came):
        slot_terms = jnp.concatenate([came[j] for j in range(len(DIRECTIONS))], axis=1)
        return exact_dot(slot_terms, placer[...], dot_t)

    row_ids = lax.broadcasted_iota(jnp.int32, (head, slots), 0)
    slot_ids = lax.broadcasted_iota(jnp.int32, (1, slots), 1)
    got_out.wait()
    got_counts.wait()
    for j in range(len(DIRECTIONS)):
        wanted = jnp.where(slot_ids < out_counts[:, j : j + 1], out_rows[j : j + 1, :], -1)
        picker[:, j * slots : (j + 1) * slots] = (row_ids == wanted).astype(jnp.bfloat16)
    got_start.wait()
    got_orders.wait()
    column_ids = lax.broadcasted_iota(jnp.int32, (1, order_pad), 1)
    row_mask = (column_ids < orders[...]).astype(jnp.float32)
    iterate = start[...] * row_mask
    iterate_bf = iterate.astype(jnp.bfloat16)
    got_head.wait()
    product_head = dot(iterate_bf, stiff[:, :head])
    picked = exact_dot(product_head, picker[...])
    for j in range(len(DIRECTIONS)):
        sent_first[j] = picked[:, j * slots : (j + 1) * slots]
    pl.semaphore_wait(barrier, devices - 1)
    moves_first = exchange(sent_first, came_first, send_first, recv_first)

    got_in.wait()
    for j in range(len(DIRECTIONS)):
        placer[:, j * slots : (j + 1) * slots] = (row_ids == in_rows[j : j + 1, :]).astype(jnp.bfloat16)
    got_rhs.wait()
    got_tail.wait()
    residual_tail = row_mask[:, head:] * (rhs[:, head:] - dot(iterate_bf, stiff[:, head:]))
    residual_out[:, head:] = residual_tail
    tail_bf = residual_tail.astype(jnp.bfloat16)
    got_basis.wait()
    basis_pad[...] = jnp.zeros_like(basis_pad)
    basis_pad[:vectors, :] = basis[...]
    coarse_tail = dot_t(tail_bf, basis_pad[:, head:])
    got_inverse.wait()
    fix_tail = dot(tail_bf, inverse[head:, :])
    got_weights.wait()
    scale = weights[...] * row_mask
    scaled_basis = scale * basis[...].astype(jnp.float32)
    picked_basis = exact_dot(scaled_basis[:, :head], picker[...])

    got_coarse.wait()
    group = math.lcm(vectors, LANES) // vectors
    lane_ids = lax.broadcasted_iota(jnp.int32, (vectors, LANES), 1)

    def spread(block, carry):
        base = pl.multiple_of(block * group * vectors, LANES)
        tiles = [
            coarse[:, pl.ds(base + t * LANES, LANES)] for t in range(group * vectors // LANES)
        ]
        for r in range(group):
            tile, first = divmod(r * vectors, LANES)
            moved = pltpu.roll(tiles[tile], LANES - first, 1) if first else tiles[tile]
            if first + vectors > LANES:
                following = pltpu.roll(tiles[tile + 1], LANES - first, 1)
                moved = jnp.where(lane_ids < LANES - first, moved, following)
            coarse_pad[block * group + r] = jnp.where(lane_ids < vectors, moved, 0.0)
        return carry

    lax.fori_loop(0, devices // group, spread, 0)

    wait_arrivals(moves_first)
    residual_head = row_mask[:, :head] * (rhs[:, :head] - (product_head + arrived_rows(came_first)))
    head_bf = residual_head.astype(jnp.bfloat16)
    gathered[me] = coarse_tail + dot_t(head_bf, basis_pad[:, :head])

    def send_coarse(step):
        return pltpu.make_async_remote_copy(
            src_ref=gathered.at[me],
            dst_ref=gathered.at[me],
            send_sem=gather_send,
            recv_sem=gather_recv,
            device_id=device_of(step),
            device_id_type=MESH,
        )

    def start_coarse(step, carry):
        send_coarse(step).start()
        return carry

    lax.fori_loop(1, devices, start_coarse, 0)

    residual_out[:, :head] = residual_head
    put_residual = pltpu.make_async_copy(residual_out, residual_hbm, store_sems.at[0])
    put_residual.start()
    fixed = scale * (fix_tail + dot(head_bf, inverse[:head, :]))
    picked_fix = exact_dot(fixed[:, :head], picker[...])
    base_out = iterate + fixed

    others = gathered.at[pl.ds(0, devices - 1)]
    pltpu.make_async_copy(others, others, gather_recv).wait()

    def accumulate(block, sums):
        sums = list(sums)
        for r in range(group):
            d = block * group + r
            terms, rows = gathered[d], coarse_pad[d]
            for l in range(loads):
                sums[l] = sums[l] + terms[l : l + 1, :] * rows
        return tuple(sums)

    sums = tuple(jnp.zeros((vectors, LANES), jnp.float32) for _ in range(loads))
    if devices // group <= 4:
        for block in range(devices // group):
            sums = accumulate(block, sums)
    else:
        sums = lax.fori_loop(0, devices // group, accumulate, sums)
    coarse_columns = [
        jnp.sum(s, axis=1, keepdims=True).astype(jnp.bfloat16).astype(jnp.float32) for s in sums
    ]

    def spanned(block):
        return jnp.concatenate(
            [jnp.sum(c * block, axis=0, keepdims=True) for c in coarse_columns], axis=0
        )

    picked = picked_fix + spanned(picked_basis)
    for j in range(len(DIRECTIONS)):
        sent_second[j] = picked[:, j * slots : (j + 1) * slots]
    moves_second = exchange(sent_second, came_second, send_second, recv_second)

    base_out = base_out + spanned(scaled_basis)
    solution_out[:, head:] = base_out[:, head:]
    wait_arrivals(moves_second)
    solution_out[:, :head] = base_out[:, :head] + arrived_rows(came_second)
    put_solution = pltpu.make_async_copy(solution_out, solution_hbm, store_sems.at[1])
    put_solution.start()

    for copy, sends, _ in moves_first + moves_second:
        pl.when(sends)(copy.wait_send)
    pltpu.make_async_copy(others, others, gather_send).wait()
    put_residual.wait()
    put_solution.wait()


def per_device(
    n_dom,
    n_sub,
    rhs,
    start,
    stiffness,
    local_inverse,
    basis,
    weights,
    coarse_inverse,
    orders,
    out_rows,
    out_counts,
    in_rows,
):
    loads, order_pad = rhs.shape
    directions, slots = out_rows.shape[1:]
    vectors = basis.shape[0]
    devices = n_dom * n_sub
    head = -(-(order_pad // 4) // LANES) * LANES
    operands = (
        rhs,
        start,
        stiffness,
        local_inverse,
        basis,
        weights.reshape(1, order_pad),
        coarse_inverse,
        orders.reshape(1, 1),
        out_rows.reshape(directions, slots),
        out_counts,
        in_rows.reshape(directions, slots),
    )
    f32 = jnp.float32
    shared = pltpu.VMEM((directions, loads, slots), f32)
    dma = pltpu.SemaphoreType.DMA
    any_space = pl.BlockSpec(memory_space=pl.ANY)
    field = jax.ShapeDtypeStruct((loads, order_pad), f32)
    return pl.pallas_call(
        functools.partial(kernel, n_dom, n_sub),
        out_shape=(field, field),
        in_specs=[any_space] * len(operands),
        out_specs=(any_space, any_space),
        scratch_shapes=[pltpu.VMEM(x.shape, x.dtype) for x in operands]
        + [
            pltpu.VMEM((head, directions * slots), jnp.bfloat16),
            pltpu.VMEM((head, directions * slots), jnp.bfloat16),
            pltpu.VMEM((LANES, order_pad), jnp.bfloat16),
            pltpu.VMEM((devices, vectors, LANES), f32),
            shared,
            shared,
            shared,
            shared,
            pltpu.VMEM((devices, loads, LANES), f32),
            pltpu.VMEM((loads, order_pad), f32),
            pltpu.VMEM((loads, order_pad), f32),
            dma((12,)),
            dma((2,)),
            dma((directions,)),
            dma((directions,)),
            dma((directions,)),
            dma((directions,)),
            dma,
            dma,
        ],
        compiler_params=pltpu.CompilerParams(
            collective_id=0, has_side_effects=True, vmem_limit_bytes=40 * 1024 * 1024
        ),
    )(*operands)


def solution(mesh):
    return jax.shard_map(
        functools.partial(per_device, mesh.shape["dom"], mesh.shape["sub"]),
        mesh=mesh,
        in_specs=(
            P(None, ("dom", "sub")),
            P(None, ("dom", "sub")),
            P(("dom", "sub"), None),
            P(("dom", "sub"), None),
            P(None, ("dom", "sub")),
            P(("dom", "sub")),
            P(("dom", "sub"), None),
            P(("dom", "sub")),
            P(("dom", "sub"), None, None),
            P(("dom", "sub"), None),
            P(("dom", "sub"), None, None),
        ),
        out_specs=(P(None, ("dom", "sub")), P(None, ("dom", "sub"))),
        check_vma=False,
    )
```

time: 95.7 us -> 28 us (0.29)
  starting transfers between devices: 31.8 us -> 0 us
  blocking collectives: 25.5 us -> 0 us
  other arithmetic: 22.5 us -> 0 us
  Pallas kernels: 0 us -> 17.5 us
  local copies, waits for them, and re-layouts: 10.8 us -> 8.81 us
  matrix products: 1.99 us -> 0 us
    ppermute x12 -> x0, starting transfers between devices: 31.8 us -> none  [passed_along(): return lax.ppermute(block, axis, route)]
    all_gather x2 -> x0, blocking collectives: 25.5 us -> none  [the longest x1 20.6 us: per_device(): lax.all_gather(grouped, 'dom', axis=1, tiled=True)]
    pallas_call x0 -> x1, Pallas kernels: none -> 17.5 us  [per_device(): pl.pallas_call(functools.partial(kernel, n_dom, n_sub), out_shape=(field,...]
    scatter-add x12 -> x0, other arithmetic: 17 us -> none  [assemble(): summed = summed.at[:, in_rows[0, index_dir]].add(arrived)]
    gather x12 -> x0, local copies, waits for them, and re-layouts: 7.75 us -> none  [assemble(): picked = terms[:, out_rows[0, index_dir]] * used[None, :]]
    unnamed x21 -> x17, local copies, waits for them, and re-layouts: 0.97 us -> 8.12 us
    convert_element_type x7 -> x0, other arithmetic: 3.78 us -> none  [the longest x6 3.78 us: assemble(): used = (slot_ids < out_counts[0, index_dir]).astype(jnp.float32)]
    dot_general x5 -> x0, matrix products: 1.99 us -> none  [the longest x1 1.29 us: per_device(): product = jnp.dot(iterate_bf, stiffness, preferred_element_type=jnp.float32)]
  transfers between devices with their start and end apart: 12 -> 0, of which waited for: 0 -> 0; matrix products, arithmetic and copies ran while one was open for 22% -> 0% of each run, Pallas kernels for 0% -> 0%
where the time goes in v1:
time: 28 us; the launch traced here: 27.6 us
  Pallas kernels  17.5 us (62%)
  local copies, waits for them, and re-layouts  8.81 us (31%)
  between operations  1.29 us (5%)
    pallas_call x1, Pallas kernels, per_device(): pl.pallas_call(functools.partial(kernel, n_dom, n_sub), out_shape=(field,...  17.5 us
    unnamed x17, local copies, waits for them, and re-layouts  8.12 us
    reshape x1, local copies, waits for them, and re-layouts, per_device(): weights.reshape(1, order_pad)  0.69 us

profile of v1, /device:TPU:0, one launch (start us, length us, event | category | flops | bytes accessed | tf_op | source)
XLA Modules:
  0.0 27.6 jit_solution(13837470632606790265)
XLA Ops:
  1.3 0.7 %reshape.16.weights_hbm = f32[1,768]{1,0:T(1,128)S(1)} reshape(f32[768]{0:T(1024)} %param.16) | data formatting | bytes 6144 | tf_op jit(solution)/shard_map/reshape | solution.py:311
  2.0 0.7 %copy_bitcast_fusion = (s32[6,128]{1,0:T(8,128)S(1)}, s32[6,128]{1,0:T(8,128)S(1)}) fusion(s32[1,6,128]{2,0,1:T(1,128)} %param.21, s32[1,6,128]{2,0,1:T(1,128)} %param.19), kind=kLoop, calls=%fused_computation | loop fusion | bytes 12288
  2.7 0.0 copy-start
  2.7 1.3 %copy-done = bf16[768,768]{1,0:T(8,128)(2,1)S(1)} copy-done((bf16[768,768]{1,0:T(8,128)(2,1)S(1)}, bf16[768,768]{1,0:T(8,128)(2,1)}, u32[]{:S(2)}) %copy-start) | copy-done | bytes 1179672
  3.9 0.0 copy-start.1
  3.9 1.3 %copy-done.1 = bf16[768,768]{1,0:T(8,128)(2,1)S(1)} copy-done((bf16[768,768]{1,0:T(8,128)(2,1)S(1)}, bf16[768,768]{1,0:T(8,128)(2,1)}, u32[]{:S(2)}) %copy-start.1) | copy-done | bytes 1179672
  5.2 0.0 copy-start.2
  5.2 0.9 %copy-done.2 = f32[24,768]{1,0:T(8,128)S(1)} copy-done((f32[24,768]{1,0:T(8,128)S(1)}, f32[24,768]{1,0:T(8,128)}, u32[]{:S(2)}) %copy-start.2) | copy-done | bytes 73752
  6.1 0.0 copy-start.3
  6.1 0.8 %copy-done.3 = bf16[24,768]{1,0:T(8,128)(2,1)S(1)} copy-done((bf16[24,768]{1,0:T(8,128)(2,1)S(1)}, bf16[24,768]{1,0:T(8,128)(2,1)}, u32[]{:S(2)}) %copy-start.3) | copy-done | bytes 36888
  6.9 0.0 copy-start.4
  6.9 0.7 %copy-done.4 = f32[2,768]{1,0:T(2,128)S(1)} copy-done((f32[2,768]{1,0:T(2,128)S(1)}, f32[2,768]{1,0:T(2,128)}, u32[]{:S(2)}) %copy-start.4) | copy-done | bytes 6168
  7.6 0.0 copy-start.5
  7.6 0.7 %copy-done.5 = f32[2,768]{1,0:T(2,128)S(1)} copy-done((f32[2,768]{1,0:T(2,128)S(1)}, f32[2,768]{1,0:T(2,128)}, u32[]{:S(2)}) %copy-start.5) | copy-done | bytes 6168
  8.2 0.0 copy-start.6
  8.3 0.7 %copy-done.6 = s32[1,6]{1,0:T(1,128)S(1)} copy-done((s32[1,6]{1,0:T(1,128)S(1)}, s32[1,6]{1,0:T(1,128)}, u32[]{:S(2)}) %copy-start.6) | copy-done | bytes 48
  8.9 17.5 %shard_map.122 = (f32[2,768]{1,0:T(2,128)S(1)}, f32[2,768]{1,0:T(2,128)S(1)}) custom-call(f32[2,768]{1,0:T(2,128)S(1)} %copy-done.4, f32[2,768]{1,0:T(2,128)S(1)} %copy-done.5, bf16[768,768]{1,0:T(8,128)(2,1)S(1)} %copy-done, bf16[768,768]{1,0:T(8,128)(2,1)S(1)} %copy-done.1, bf16[24,768]{1,0:T(8,128)(2,1)S(1)} %copy-done.3, ...), custom_call_target="tpu_custom_call" | custom-call | tf_op jit(solution)/shard_map/pallas_call | solution.py:323
  26.4 0.6 %copy.20 = f32[2,768]{1,0:T(2,128)} copy(f32[2,768]{1,0:T(2,128)S(1)} %get-tuple-element.6) | data formatting | bytes 12288
  27.0 0.6 %copy.21 = f32[2,768]{1,0:T(2,128)} copy(f32[2,768]{1,0:T(2,128)S(1)} %get-tuple-element.7) | data formatting | bytes 12288
Async XLA Ops:
  2.7 1.3 %copy-start = (bf16[768,768]{1,0:T(8,128)(2,1)S(1)}, bf16[768,768]{1,0:T(8,128)(2,1)}, u32[]{:S(2)}) copy-start(bf16[768,768]{1,0:T(8,128)(2,1)} %stiff_hbm.1) | copy-start | bytes 3538948
  3.9 1.3 %copy-start.1 = (bf16[768,768]{1,0:T(8,128)(2,1)S(1)}, bf16[768,768]{1,0:T(8,128)(2,1)}, u32[]{:S(2)}) copy-start(bf16[768,768]{1,0:T(8,128)(2,1)} %inverse_hbm.1) | copy-start | bytes 3538948
  5.2 0.9 %copy-start.2 = (f32[24,768]{1,0:T(8,128)S(1)}, f32[24,768]{1,0:T(8,128)}, u32[]{:S(2)}) copy-start(f32[24,768]{1,0:T(8,128)} %coarse_hbm.1) | copy-start | bytes 221188
  6.1 0.8 %copy-start.3 = (bf16[24,768]{1,0:T(8,128)(2,1)S(1)}, bf16[24,768]{1,0:T(8,128)(2,1)}, u32[]{:S(2)}) copy-start(bf16[24,768]{1,0:T(8,128)(2,1)} %basis_hbm.1) | copy-start | bytes 110596
  6.9 0.7 %copy-start.4 = (f32[2,768]{1,0:T(2,128)S(1)}, f32[2,768]{1,0:T(2,128)}, u32[]{:S(2)}) copy-start(f32[2,768]{1,0:T(2,128)} %rhs_hbm.1) | copy-start | bytes 18436
  7.6 0.7 %copy-start.5 = (f32[2,768]{1,0:T(2,128)S(1)}, f32[2,768]{1,0:T(2,128)}, u32[]{:S(2)}) copy-start(f32[2,768]{1,0:T(2,128)} %start_hbm.1) | copy-start | bytes 18436
  8.2 0.7 %copy-start.6 = (s32[1,6]{1,0:T(1,128)S(1)}, s32[1,6]{1,0:T(1,128)}, u32[]{:S(2)}) copy-start(s32[1,6]{1,0:T(1,128)} %out_counts_hbm.1) | copy-start | bytes 76

commit v2 on v1

--- a/solution.py
+++ b/solution.py
@@ -35,6 +35,7 @@
 def kernel(
     n_dom,
     n_sub,
+    team,
     rhs_hbm,
     start_hbm,
     stiff_hbm,
@@ -76,12 +77,14 @@
     recv_first,
     send_second,
     recv_second,
-    gather_send,
-    gather_recv,
+    team_send,
+    team_recv,
+    column_send,
+    column_recv,
 ):
     devices = n_dom * n_sub
     loads, order_pad = rhs.shape
-    slots = out_rows.shape[1]
+    slots = out_rows.shape[2]
     vectors = basis.shape[0]
     head = placer.shape[0]
     dom, sub = lax.axis_index("dom"), lax.axis_index("sub")
@@ -93,32 +96,54 @@
         return copy
 
     got_start = load(0, start_hbm, start)
+    got_head = load(2, stiff_hbm.at[:, :head], stiff.at[:, :head])
     got_orders = load(1, orders_hbm, orders)
-    got_head = load(2, stiff_hbm.at[:, :head], stiff.at[:, :head])
     got_out = load(3, out_rows_hbm, out_rows)
     got_counts = load(4, out_counts_hbm, out_counts)
+
+    came_first[...] = jnp.zeros_like(came_first)
+    came_second[...] = jnp.zeros_like(came_second)
+
+    teams = n_dom // team
+    place = lax.rem(dom, team)
+    team_first = dom - place
+    column_id = lax.div(dom, team)
+
+    def wrapped(index, size):
+        return jnp.where(index >= size, index - size, index)
+
+    def team_mate(step):
+        along, across = divmod(step, n_sub)
+        return (team_first + wrapped(place + along, team), wrapped(sub + across, n_sub))
+
+    def column_mate(step):
+        return (wrapped(column_id + step, teams) * team + place, sub)
+
+    team_steps, column_steps = range(1, team * n_sub), range(1, teams)
+    far = [offset for axis_name, offset in DIRECTIONS if axis_name == "dom"]
+
+    barrier = pltpu.get_barrier_semaphore()
+
+    def greet(device):
+        pl.semaphore_signal(barrier, inc=1, device_id=device, device_id_type=MESH)
+
+    greetings = len(team_steps) + len(column_steps)
+    for step in column_steps:
+        greet(column_mate(step))
+    for offset in far:
+        inside = (dom + offset >= 0) & (dom + offset < n_dom)
+        pl.when(inside)(functools.partial(greet, (dom + offset, sub)))
+        greetings = greetings + inside.astype(jnp.int32)
+    for step in team_steps:
+        greet(team_mate(step))
+
     got_tail = load(5, stiff_hbm.at[:, head:], stiff.at[:, head:])
     got_in = load(6, in_rows_hbm, in_rows)
     got_rhs = load(7, rhs_hbm, rhs)
     got_basis = load(8, basis_hbm, basis)
+    got_inverse = load(10, inverse_hbm, inverse)
     got_weights = load(9, weights_hbm, weights)
-    got_inverse = load(10, inverse_hbm, inverse)
     got_coarse = load(11, coarse_hbm, coarse)
-
-    came_first[...] = jnp.zeros_like(came_first)
-    came_second[...] = jnp.zeros_like(came_second)
-
-    barrier = pltpu.get_barrier_semaphore()
-
-    def device_of(step):
-        peer = lax.rem(me + step, devices)
-        return (lax.div(peer, n_sub), lax.rem(peer, n_sub))
-
-    def greet(step, carry):
-        pl.semaphore_signal(barrier, inc=1, device_id=device_of(step), device_id_type=MESH)
-        return carry
-
-    lax.fori_loop(1, devices, greet, 0)
 
     def exchange(sent, came, send_sems, recv_sems):
         moves = []
@@ -153,7 +178,7 @@
     got_out.wait()
     got_counts.wait()
     for j in range(len(DIRECTIONS)):
-        wanted = jnp.where(slot_ids < out_counts[:, j : j + 1], out_rows[j : j + 1, :], -1)
+        wanted = jnp.where(slot_ids < out_counts[:, j : j + 1], out_rows[j], -1)
         picker[:, j * slots : (j + 1) * slots] = (row_ids == wanted).astype(jnp.bfloat16)
     got_start.wait()
     got_orders.wait()
@@ -166,12 +191,12 @@
     picked = exact_dot(product_head, picker[...])
     for j in range(len(DIRECTIONS)):
         sent_first[j] = picked[:, j * slots : (j + 1) * slots]
-    pl.semaphore_wait(barrier, devices - 1)
+    pl.semaphore_wait(barrier, greetings)
     moves_first = exchange(sent_first, came_first, send_first, recv_first)
 
     got_in.wait()
     for j in range(len(DIRECTIONS)):
-        placer[:, j * slots : (j + 1) * slots] = (row_ids == in_rows[j : j + 1, :]).astype(jnp.bfloat16)
+        placer[:, j * slots : (j + 1) * slots] = (row_ids == in_rows[j]).astype(jnp.bfloat16)
     got_rhs.wait()
     got_tail.wait()
     residual_tail = row_mask[:, head:] * (rhs[:, head:] - dot(iterate_bf, stiff[:, head:]))
@@ -183,8 +208,43 @@
     coarse_tail = dot_t(tail_bf, basis_pad[:, head:])
     got_inverse.wait()
     fix_tail = dot(tail_bf, inverse[head:, :])
+
+    wait_arrivals(moves_first)
+    residual_head = row_mask[:, :head] * (rhs[:, :head] - (product_head + arrived_rows(came_first)))
+    head_bf = residual_head.astype(jnp.bfloat16)
+    gathered[me] = coarse_tail + dot_t(head_bf, basis_pad[:, :head])
+
+    def share(slabs, device, send_sem, recv_sem):
+        pltpu.make_async_remote_copy(
+            src_ref=gathered.at[slabs],
+            dst_ref=gathered.at[slabs],
+            send_sem=send_sem,
+            recv_sem=recv_sem,
+            device_id=device,
+            device_id_type=MESH,
+        ).start()
+
+    def wait_slabs(count, sem):
+        some = gathered.at[pl.ds(0, count)]
+        pltpu.make_async_copy(some, some, sem).wait()
+
+    for step in team_steps:
+        share(pl.ds(me, 1), team_mate(step), team_send, team_recv)
+
+    residual_out[:, :head] = residual_head
+    put_residual = pltpu.make_async_copy(residual_out, residual_hbm, store_sems.at[0])
+    put_residual.start()
     got_weights.wait()
-    scale = weights[...] * row_mask
+    scale = weights[...].reshape(1, order_pad) * row_mask
+    fixed = scale * (fix_tail + dot(head_bf, inverse[:head, :]))
+    picked_fix = exact_dot(fixed[:, :head], picker[...])
+    base_out = iterate + fixed
+
+    mates = team * n_sub
+    wait_slabs(mates - 1, team_recv)
+    for step in column_steps:
+        share(pl.ds(team_first * n_sub, mates), column_mate(step), column_send, column_recv)
+
     scaled_basis = scale * basis[...].astype(jnp.float32)
     picked_basis = exact_dot(scaled_basis[:, :head], picker[...])
 
@@ -208,36 +268,7 @@
 
     lax.fori_loop(0, devices // group, spread, 0)
 
-    wait_arrivals(moves_first)
-    residual_head = row_mask[:, :head] * (rhs[:, :head] - (product_head + arrived_rows(came_first)))
-    head_bf = residual_head.astype(jnp.bfloat16)
-    gathered[me] = coarse_tail + dot_t(head_bf, basis_pad[:, :head])
-
-    def send_coarse(step):
-        return pltpu.make_async_remote_copy(
-            src_ref=gathered.at[me],
-            dst_ref=gathered.at[me],
-            send_sem=gather_send,
-            recv_sem=gather_recv,
-            device_id=device_of(step),
-            device_id_type=MESH,
-        )
-
-    def start_coarse(step, carry):
-        send_coarse(step).start()
-        return carry
-
-    lax.fori_loop(1, devices, start_coarse, 0)
-
-    residual_out[:, :head] = residual_head
-    put_residual = pltpu.make_async_copy(residual_out, residual_hbm, store_sems.at[0])
-    put_residual.start()
-    fixed = scale * (fix_tail + dot(head_bf, inverse[:head, :]))
-    picked_fix = exact_dot(fixed[:, :head], picker[...])
-    base_out = iterate + fixed
-
-    others = gathered.at[pl.ds(0, devices - 1)]
-    pltpu.make_async_copy(others, others, gather_recv).wait()
+    wait_slabs(devices - mates, column_recv)
 
     def accumulate(block, sums):
         sums = list(sums)
@@ -277,7 +308,8 @@
 
     for copy, sends, _ in moves_first + moves_second:
         pl.when(sends)(copy.wait_send)
-    pltpu.make_async_copy(others, others, gather_send).wait()
+    wait_slabs(mates - 1, team_send)
+    wait_slabs(devices - mates, column_send)
     put_residual.wait()
     put_solution.wait()
 
@@ -299,6 +331,7 @@
 ):
     loads, order_pad = rhs.shape
     directions, slots = out_rows.shape[1:]
+    team = min(t for t in range(1, n_dom + 1) if n_dom % t == 0 and t * t * n_sub >= n_dom)
     vectors = basis.shape[0]
     devices = n_dom * n_sub
     head = -(-(order_pad // 4) // LANES) * LANES
@@ -308,23 +341,23 @@
         stiffness,
         local_inverse,
         basis,
-        weights.reshape(1, order_pad),
+        weights,
         coarse_inverse,
         orders.reshape(1, 1),
-        out_rows.reshape(directions, slots),
+        out_rows.transpose(1, 0, 2),
         out_counts,
-        in_rows.reshape(directions, slots),
+        in_rows.transpose(1, 0, 2),
     )
     f32 = jnp.float32
     shared = pltpu.VMEM((directions, loads, slots), f32)
     dma = pltpu.SemaphoreType.DMA
-    any_space = pl.BlockSpec(memory_space=pl.ANY)
+    in_hbm = pl.BlockSpec(memory_space=pltpu.HBM)
     field = jax.ShapeDtypeStruct((loads, order_pad), f32)
     return pl.pallas_call(
-        functools.partial(kernel, n_dom, n_sub),
+        functools.partial(kernel, n_dom, n_sub, team),
         out_shape=(field, field),
-        in_specs=[any_space] * len(operands),
-        out_specs=(any_space, any_space),
+        in_specs=[in_hbm] * len(operands),
+        out_specs=(in_hbm, in_hbm),
         scratch_shapes=[pltpu.VMEM(x.shape, x.dtype) for x in operands]
         + [
             pltpu.VMEM((head, directions * slots), jnp.bfloat16),
@@ -346,9 +379,11 @@
             dma((directions,)),
             dma,
             dma,
+            dma,
+            dma,
         ],
         compiler_params=pltpu.CompilerParams(
-            collective_id=0, has_side_effects=True, vmem_limit_bytes=40 * 1024 * 1024
+            collective_id=0, has_side_effects=True, vmem_limit_bytes=63 * 1024 * 1024
         ),
     )(*operands)
 

time: 28 us -> 23.6 us (0.84)
  local copies, waits for them, and re-layouts: 8.81 us -> 2.57 us
  Pallas kernels: 17.5 us -> 19.5 us
    unnamed x17 -> x2, local copies, waits for them, and re-layouts: 8.12 us -> 2.57 us
    pallas_call x1, Pallas kernels: 17.5 us -> 19.5 us  [per_device(): pl.pallas_call(functools.partial(kernel, n_dom, n_sub, team), out_shape=(...]
    reshape x1 -> x0, local copies, waits for them, and re-layouts: 0.69 us -> none  [per_device(): weights.reshape(1, order_pad)]
where the time goes in v2:
time: 23.6 us; the launch traced here: 23.3 us
  Pallas kernels  19.5 us (83%)
  local copies, waits for them, and re-layouts  2.57 us (11%)
  between operations  1.29 us (5%)
    pallas_call x1, Pallas kernels, per_device(): pl.pallas_call(functools.partial(kernel, n_dom, n_sub, team), out_shape=(...  19.5 us
    unnamed x2, local copies, waits for them, and re-layouts  2.57 us

profile of v2, /device:TPU:0, one launch (start us, length us, event | category | flops | bytes accessed | tf_op | source)
XLA Modules:
  0.0 23.3 jit_solution(5151596180033164463)
XLA Ops:
  1.3 19.5 %shard_map.122 = (f32[2,768]{1,0:T(2,128)}, f32[2,768]{1,0:T(2,128)}) custom-call(f32[2,768]{1,0:T(2,128)} %rhs_hbm.1, f32[2,768]{1,0:T(2,128)} %start_hbm.1, bf16[768,768]{1,0:T(8,128)(2,1)} %stiff_hbm.1, bf16[768,768]{1,0:T(8,128)(2,1)} %inverse_hbm.1, bf16[24,768]{1,0:T(8,128)(2,1)} %basis_hbm.1, f32[768]{0:T(1024)} %weights_hbm.1, f32[24,768]{1,0:T(8,128)} %coarse_hbm.1, ...), custom_call_target="tpu_custom_call" | custom-call | tf_op jit(solution)/shard_map/pallas_call | solution.py:356
  20.8 1.3 %copy.16 = f32[2,768]{1,0:T(2,128)} copy(f32[2,768]{1,0:T(2,128)} %get-tuple-element.4) | data formatting | bytes 12288
  22.1 1.3 %copy.17 = f32[2,768]{1,0:T(2,128)} copy(f32[2,768]{1,0:T(2,128)} %get-tuple-element.5) | data formatting | bytes 12288

commit v3 on v2

--- a/solution.py
+++ b/solution.py
@@ -47,8 +47,7 @@
     out_rows_hbm,
     out_counts_hbm,
     in_rows_hbm,
-    solution_hbm,
-    residual_hbm,
+    results_hbm,
     rhs,
     start,
     stiff,
@@ -63,16 +62,16 @@
     picker,
     placer,
     basis_pad,
+    slot_basis,
     coarse_pad,
     sent_first,
     sent_second,
     came_first,
     came_second,
     gathered,
-    solution_out,
-    residual_out,
+    results,
     load_sems,
-    store_sems,
+    store_sem,
     send_first,
     recv_first,
     send_second,
@@ -86,7 +85,7 @@
     loads, order_pad = rhs.shape
     slots = out_rows.shape[2]
     vectors = basis.shape[0]
-    head = placer.shape[0]
+    head = placer.shape[1]
     dom, sub = lax.axis_index("dom"), lax.axis_index("sub")
     me = dom * n_sub + sub
 
@@ -100,6 +99,7 @@
     got_orders = load(1, orders_hbm, orders)
     got_out = load(3, out_rows_hbm, out_rows)
     got_counts = load(4, out_counts_hbm, out_counts)
+    got_in = load(6, in_rows_hbm, in_rows)
 
     came_first[...] = jnp.zeros_like(came_first)
     came_second[...] = jnp.zeros_like(came_second)
@@ -138,7 +138,6 @@
         greet(team_mate(step))
 
     got_tail = load(5, stiff_hbm.at[:, head:], stiff.at[:, head:])
-    got_in = load(6, in_rows_hbm, in_rows)
     got_rhs = load(7, rhs_hbm, rhs)
     got_basis = load(8, basis_hbm, basis)
     got_inverse = load(10, inverse_hbm, inverse)
@@ -169,9 +168,8 @@
         for copy, _, receives in moves:
             pl.when(receives)(copy.wait_recv)
 
-    def arrived_rows(came):
-        slot_terms = jnp.concatenate([came[j] for j in range(len(DIRECTIONS))], axis=1)
-        return exact_dot(slot_terms, placer[...], dot_t)
+    def arrived_slots(came):
+        return jnp.concatenate([came[j] for j in range(len(DIRECTIONS))], axis=1)
 
     row_ids = lax.broadcasted_iota(jnp.int32, (head, slots), 0)
     slot_ids = lax.broadcasted_iota(jnp.int32, (1, slots), 1)
@@ -180,6 +178,14 @@
     for j in range(len(DIRECTIONS)):
         wanted = jnp.where(slot_ids < out_counts[:, j : j + 1], out_rows[j], -1)
         picker[:, j * slots : (j + 1) * slots] = (row_ids == wanted).astype(jnp.bfloat16)
+    got_in.wait()
+    place_ids = lax.broadcasted_iota(jnp.int32, (slots, slots), 1)
+    for j in range(len(DIRECTIONS)):
+        listed = jnp.broadcast_to(in_rows[j].astype(jnp.float32), (slots, slots)).T
+        for t in range(head // slots):
+            placer[j * slots : (j + 1) * slots, t * slots : (t + 1) * slots] = (
+                listed == (place_ids + t * slots).astype(jnp.float32)
+            ).astype(jnp.bfloat16)
     got_start.wait()
     got_orders.wait()
     column_ids = lax.broadcasted_iota(jnp.int32, (1, order_pad), 1)
@@ -194,25 +200,26 @@
     pl.semaphore_wait(barrier, greetings)
     moves_first = exchange(sent_first, came_first, send_first, recv_first)
 
-    got_in.wait()
-    for j in range(len(DIRECTIONS)):
-        placer[:, j * slots : (j + 1) * slots] = (row_ids == in_rows[j]).astype(jnp.bfloat16)
     got_rhs.wait()
     got_tail.wait()
     residual_tail = row_mask[:, head:] * (rhs[:, head:] - dot(iterate_bf, stiff[:, head:]))
-    residual_out[:, head:] = residual_tail
+    results[1, :, head:] = residual_tail
     tail_bf = residual_tail.astype(jnp.bfloat16)
     got_basis.wait()
     basis_pad[...] = jnp.zeros_like(basis_pad)
     basis_pad[:vectors, :] = basis[...]
-    coarse_tail = dot_t(tail_bf, basis_pad[:, head:])
+    slot_basis[...] = dot_t(
+        placer[...], basis_pad[:, :head] * row_mask[:, :head].astype(jnp.bfloat16)
+    ).astype(jnp.bfloat16)
+    own_head = row_mask[:, :head] * (rhs[:, :head] - product_head)
+    own_residual = jnp.concatenate([own_head, residual_tail], axis=1)
+    own_coarse = exact_dot(own_residual, basis_pad[...], dot_t)
     got_inverse.wait()
     fix_tail = dot(tail_bf, inverse[head:, :])
 
     wait_arrivals(moves_first)
-    residual_head = row_mask[:, :head] * (rhs[:, :head] - (product_head + arrived_rows(came_first)))
-    head_bf = residual_head.astype(jnp.bfloat16)
-    gathered[me] = coarse_tail + dot_t(head_bf, basis_pad[:, :head])
+    arrived = arrived_slots(came_first)
+    gathered[me] = own_coarse - exact_dot(arrived, slot_basis[...])
 
     def share(slabs, device, send_sem, recv_sem):
         pltpu.make_async_remote_copy(
@@ -231,9 +238,9 @@
     for step in team_steps:
         share(pl.ds(me, 1), team_mate(step), team_send, team_recv)
 
-    residual_out[:, :head] = residual_head
-    put_residual = pltpu.make_async_copy(residual_out, residual_hbm, store_sems.at[0])
-    put_residual.start()
+    residual_head = own_head - row_mask[:, :head] * exact_dot(arrived, placer[...])
+    head_bf = residual_head.astype(jnp.bfloat16)
+    results[1, :, :head] = residual_head
     got_weights.wait()
     scale = weights[...].reshape(1, order_pad) * row_mask
     fixed = scale * (fix_tail + dot(head_bf, inverse[:head, :]))
@@ -300,18 +307,18 @@
     moves_second = exchange(sent_second, came_second, send_second, recv_second)
 
     base_out = base_out + spanned(scaled_basis)
-    solution_out[:, head:] = base_out[:, head:]
+    results[0, :, head:] = base_out[:, head:]
     wait_arrivals(moves_second)
-    solution_out[:, :head] = base_out[:, :head] + arrived_rows(came_second)
-    put_solution = pltpu.make_async_copy(solution_out, solution_hbm, store_sems.at[1])
-    put_solution.start()
+    placed = exact_dot(arrived_slots(came_second), placer[...])
+    results[0, :, :head] = base_out[:, :head] + placed
+    put_results = pltpu.make_async_copy(results, results_hbm, store_sem)
+    put_results.start()
 
     for copy, sends, _ in moves_first + moves_second:
         pl.when(sends)(copy.wait_send)
     wait_slabs(mates - 1, team_send)
     wait_slabs(devices - mates, column_send)
-    put_residual.wait()
-    put_solution.wait()
+    put_results.wait()
 
 
 def per_device(
@@ -352,27 +359,27 @@
     shared = pltpu.VMEM((directions, loads, slots), f32)
     dma = pltpu.SemaphoreType.DMA
     in_hbm = pl.BlockSpec(memory_space=pltpu.HBM)
-    field = jax.ShapeDtypeStruct((loads, order_pad), f32)
-    return pl.pallas_call(
+    both = jax.ShapeDtypeStruct((2, loads, order_pad), f32)
+    results = pl.pallas_call(
         functools.partial(kernel, n_dom, n_sub, team),
-        out_shape=(field, field),
+        out_shape=both,
         in_specs=[in_hbm] * len(operands),
-        out_specs=(in_hbm, in_hbm),
+        out_specs=in_hbm,
         scratch_shapes=[pltpu.VMEM(x.shape, x.dtype) for x in operands]
         + [
             pltpu.VMEM((head, directions * slots), jnp.bfloat16),
-            pltpu.VMEM((head, directions * slots), jnp.bfloat16),
+            pltpu.VMEM((directions * slots, head), jnp.bfloat16),
             pltpu.VMEM((LANES, order_pad), jnp.bfloat16),
+            pltpu.VMEM((directions * slots, LANES), jnp.bfloat16),
             pltpu.VMEM((devices, vectors, LANES), f32),
             shared,
             shared,
             shared,
             shared,
             pltpu.VMEM((devices, loads, LANES), f32),
-            pltpu.VMEM((loads, order_pad), f32),
-            pltpu.VMEM((loads, order_pad), f32),
+            pltpu.VMEM((2, loads, order_pad), f32),
             dma((12,)),
-            dma((2,)),
+            dma,
             dma((directions,)),
             dma((directions,)),
             dma((directions,)),
@@ -386,6 +393,7 @@
             collective_id=0, has_side_effects=True, vmem_limit_bytes=63 * 1024 * 1024
         ),
     )(*operands)
+    return results[0], results[1]
 
 
 def solution(mesh):

time: 23.6 us -> 21.9 us (0.928)
  local copies, waits for them, and re-layouts: 2.57 us -> 1.31 us
  Pallas kernels: 19.5 us -> 19.1 us
    unnamed x2 -> x0, local copies, waits for them, and re-layouts: 2.57 us -> none
    squeeze x0 -> x1, local copies, waits for them, and re-layouts: none -> 1.31 us  [per_device(): return (results[0], results[1])]
    pallas_call x1, Pallas kernels: 19.5 us -> 19.1 us  [per_device(): pl.pallas_call(functools.partial(kernel, n_dom, n_sub, team), out_shape=b...]
where the time goes in v3:
time: 21.9 us; the launch traced here: 21.7 us
  Pallas kernels  19.1 us (87%)
  local copies, waits for them, and re-layouts  1.31 us (6%)
  between operations  1.29 us (6%)
    pallas_call x1, Pallas kernels, per_device(): pl.pallas_call(functools.partial(kernel, n_dom, n_sub, team), out_shape=b...  19.1 us
    squeeze x1, local copies, waits for them, and re-layouts, per_device(): return (results[0], results[1])  1.31 us

profile of v3, /device:TPU:0, one launch (start us, length us, event | category | flops | bytes accessed | tf_op | source)
XLA Modules:
  0.0 21.7 jit_solution(1752859173318267649)
XLA Ops:
  1.3 19.1 %shard_map.122 = f32[2,2,768]{2,1,0:T(2,128)} custom-call(f32[2,768]{1,0:T(2,128)} %rhs_hbm.1, f32[2,768]{1,0:T(2,128)} %start_hbm.1, bf16[768,768]{1,0:T(8,128)(2,1)} %stiff_hbm.1, bf16[768,768]{1,0:T(8,128)(2,1)} %inverse_hbm.1, bf16[24,768]{1,0:T(8,128)(2,1)} %basis_hbm.1, f32[768]{0:T(1024)} %weights_hbm.1, f32[24,768]{1,0:T(8,128)} %coarse_hbm.1, ...), custom_call_target="tpu_custom_call" | custom-call | tf_op jit(solution)/shard_map/pallas_call | solution.py:363
  20.4 1.3 %slice_bitcast_fusion = (f32[2,768]{1,0:T(2,128)}, f32[2,768]{1,0:T(2,128)}) fusion(f32[2,2,768]{2,1,0:T(2,128)} %shard_map.122), kind=kLoop, calls=%fused_computation | loop fusion | bytes 24576 | tf_op jit(solution)/shard_map/squeeze | solution.py:396

commit v4 on v3

--- a/solution.py
+++ b/solution.py
@@ -47,7 +47,7 @@
     out_rows_hbm,
     out_counts_hbm,
     in_rows_hbm,
-    results_hbm,
+    results,
     rhs,
     start,
     stiff,
@@ -69,9 +69,7 @@
     came_first,
     came_second,
     gathered,
-    results,
     load_sems,
-    store_sem,
     send_first,
     recv_first,
     send_second,
@@ -178,14 +176,6 @@
     for j in range(len(DIRECTIONS)):
         wanted = jnp.where(slot_ids < out_counts[:, j : j + 1], out_rows[j], -1)
         picker[:, j * slots : (j + 1) * slots] = (row_ids == wanted).astype(jnp.bfloat16)
-    got_in.wait()
-    place_ids = lax.broadcasted_iota(jnp.int32, (slots, slots), 1)
-    for j in range(len(DIRECTIONS)):
-        listed = jnp.broadcast_to(in_rows[j].astype(jnp.float32), (slots, slots)).T
-        for t in range(head // slots):
-            placer[j * slots : (j + 1) * slots, t * slots : (t + 1) * slots] = (
-                listed == (place_ids + t * slots).astype(jnp.float32)
-            ).astype(jnp.bfloat16)
     got_start.wait()
     got_orders.wait()
     column_ids = lax.broadcasted_iota(jnp.int32, (1, order_pad), 1)
@@ -200,11 +190,18 @@
     pl.semaphore_wait(barrier, greetings)
     moves_first = exchange(sent_first, came_first, send_first, recv_first)
 
+    got_in.wait()
+    place_ids = lax.broadcasted_iota(jnp.int32, (slots, slots), 1)
+    for j in range(len(DIRECTIONS)):
+        listed = jnp.broadcast_to(in_rows[j].astype(jnp.float32), (slots, slots)).T
+        for t in range(head // slots):
+            placer[j * slots : (j + 1) * slots, t * slots : (t + 1) * slots] = (
+                listed == (place_ids + t * slots).astype(jnp.float32)
+            ).astype(jnp.bfloat16)
     got_rhs.wait()
     got_tail.wait()
     residual_tail = row_mask[:, head:] * (rhs[:, head:] - dot(iterate_bf, stiff[:, head:]))
     results[1, :, head:] = residual_tail
-    tail_bf = residual_tail.astype(jnp.bfloat16)
     got_basis.wait()
     basis_pad[...] = jnp.zeros_like(basis_pad)
     basis_pad[:vectors, :] = basis[...]
@@ -214,8 +211,6 @@
     own_head = row_mask[:, :head] * (rhs[:, :head] - product_head)
     own_residual = jnp.concatenate([own_head, residual_tail], axis=1)
     own_coarse = exact_dot(own_residual, basis_pad[...], dot_t)
-    got_inverse.wait()
-    fix_tail = dot(tail_bf, inverse[head:, :])
 
     wait_arrivals(moves_first)
     arrived = arrived_slots(came_first)
@@ -239,11 +234,12 @@
         share(pl.ds(me, 1), team_mate(step), team_send, team_recv)
 
     residual_head = own_head - row_mask[:, :head] * exact_dot(arrived, placer[...])
-    head_bf = residual_head.astype(jnp.bfloat16)
+    residual_bf = jnp.concatenate([residual_head, residual_tail], axis=1).astype(jnp.bfloat16)
     results[1, :, :head] = residual_head
     got_weights.wait()
     scale = weights[...].reshape(1, order_pad) * row_mask
-    fixed = scale * (fix_tail + dot(head_bf, inverse[:head, :]))
+    got_inverse.wait()
+    fixed = scale * dot(residual_bf, inverse[...])
     picked_fix = exact_dot(fixed[:, :head], picker[...])
     base_out = iterate + fixed
 
@@ -311,14 +307,11 @@
     wait_arrivals(moves_second)
     placed = exact_dot(arrived_slots(came_second), placer[...])
     results[0, :, :head] = base_out[:, :head] + placed
-    put_results = pltpu.make_async_copy(results, results_hbm, store_sem)
-    put_results.start()
 
     for copy, sends, _ in moves_first + moves_second:
         pl.when(sends)(copy.wait_send)
     wait_slabs(mates - 1, team_send)
     wait_slabs(devices - mates, column_send)
-    put_results.wait()
 
 
 def per_device(
@@ -359,12 +352,12 @@
     shared = pltpu.VMEM((directions, loads, slots), f32)
     dma = pltpu.SemaphoreType.DMA
     in_hbm = pl.BlockSpec(memory_space=pltpu.HBM)
-    both = jax.ShapeDtypeStruct((2, loads, order_pad), f32)
+    both = pltpu.VMEM((2, loads, order_pad), f32)
     results = pl.pallas_call(
         functools.partial(kernel, n_dom, n_sub, team),
         out_shape=both,
         in_specs=[in_hbm] * len(operands),
-        out_specs=in_hbm,
+        out_specs=pl.BlockSpec(memory_space=pltpu.VMEM),
         scratch_shapes=[pltpu.VMEM(x.shape, x.dtype) for x in operands]
         + [
             pltpu.VMEM((head, directions * slots), jnp.bfloat16),
@@ -377,9 +370,7 @@
             shared,
             shared,
             pltpu.VMEM((devices, loads, LANES), f32),
-            pltpu.VMEM((2, loads, order_pad), f32),
             dma((12,)),
-            dma,
             dma((directions,)),
             dma((directions,)),
             dma((directions,)),

time: 21.9 us -> 20.6 us (0.941)
  local copies, waits for them, and re-layouts: 1.31 us -> 0.6 us
  Pallas kernels: 19.1 us -> 18.5 us
    squeeze x1, local copies, waits for them, and re-layouts: 1.31 us -> 0.6 us  [per_device(): return (results[0], results[1])]
    pallas_call x1, Pallas kernels: 19.1 us -> 18.5 us  [per_device(): pl.pallas_call(functools.partial(kernel, n_dom, n_sub, team), out_shape=b...]
where the time goes in v4:
time: 20.6 us; the launch traced here: 20.4 us
  Pallas kernels  18.5 us (90%)
  between operations  1.29 us (6%)
  local copies, waits for them, and re-layouts  0.6 us (3%)
    pallas_call x1, Pallas kernels, per_device(): pl.pallas_call(functools.partial(kernel, n_dom, n_sub, team), out_shape=b...  18.5 us
    squeeze x1, local copies, waits for them, and re-layouts, per_device(): return (results[0], results[1])  0.6 us

profile of v4, /device:TPU:0, one launch (start us, length us, event | category | flops | bytes accessed | tf_op | source)
XLA Modules:
  0.0 20.4 jit_solution(17330863949012730343)
XLA Ops:
  1.3 18.5 %shard_map.122 = f32[2,2,768]{2,1,0:T(2,128)S(1)} custom-call(f32[2,768]{1,0:T(2,128)} %rhs_hbm.1, f32[2,768]{1,0:T(2,128)} %start_hbm.1, bf16[768,768]{1,0:T(8,128)(2,1)} %stiff_hbm.1, bf16[768,768]{1,0:T(8,128)(2,1)} %inverse_hbm.1, bf16[24,768]{1,0:T(8,128)(2,1)} %basis_hbm.1, f32[768]{0:T(1024)} %weights_hbm.1, f32[24,768]{1,0:T(8,128)} %coarse_hbm.1, ...), custom_call_target="tpu_custom_call" | custom-call | tf_op jit(solution)/shard_map/pallas_call | solution.py:356
  19.8 0.6 %slice_bitcast_fusion = (f32[2,768]{1,0:T(2,128)}, f32[2,768]{1,0:T(2,128)}) fusion(f32[2,2,768]{2,1,0:T(2,128)S(1)} %shard_map.122), kind=kLoop, calls=%fused_computation | loop fusion | bytes 24576 | tf_op jit(solution)/shard_map/squeeze | solution.py:387

commit v5 on v4

--- a/solution.py
+++ b/solution.py
@@ -92,8 +92,8 @@
         copy.start()
         return copy
 
+    got_head = load(2, stiff_hbm.at[:, :head], stiff.at[:, :head])
     got_start = load(0, start_hbm, start)
-    got_head = load(2, stiff_hbm.at[:, :head], stiff.at[:, :head])
     got_orders = load(1, orders_hbm, orders)
     got_out = load(3, out_rows_hbm, out_rows)
     got_counts = load(4, out_counts_hbm, out_counts)
@@ -304,14 +304,13 @@
 
     base_out = base_out + spanned(scaled_basis)
     results[0, :, head:] = base_out[:, head:]
-    wait_arrivals(moves_second)
-    placed = exact_dot(arrived_slots(came_second), placer[...])
-    results[0, :, :head] = base_out[:, :head] + placed
-
     for copy, sends, _ in moves_first + moves_second:
         pl.when(sends)(copy.wait_send)
     wait_slabs(mates - 1, team_send)
     wait_slabs(devices - mates, column_send)
+    wait_arrivals(moves_second)
+    placed = exact_dot(arrived_slots(came_second), placer[...])
+    results[0, :, :head] = base_out[:, :head] + placed
 
 
 def per_device(

time: 20.6 us -> 20.6 us (level)
  no operation moved by 1% of the time
where the time goes in v5:
time: 20.6 us; the launch traced here: 20.4 us
  Pallas kernels  18.5 us (90%)
  between operations  1.29 us (6%)
  local copies, waits for them, and re-layouts  0.6 us (3%)
    pallas_call x1, Pallas kernels, per_device(): pl.pallas_call(functools.partial(kernel, n_dom, n_sub, team), out_shape=b...  18.5 us
    squeeze x1, local copies, waits for them, and re-layouts, per_device(): return (results[0], results[1])  0.6 us

profile of v5, /device:TPU:0, one launch (start us, length us, event | category | flops | bytes accessed | tf_op | source)
XLA Modules:
  0.0 20.4 jit_solution(3905983322639732084)
XLA Ops:
  1.3 18.5 %shard_map.122 = f32[2,2,768]{2,1,0:T(2,128)S(1)} custom-call(f32[2,768]{1,0:T(2,128)} %rhs_hbm.1, f32[2,768]{1,0:T(2,128)} %start_hbm.1, bf16[768,768]{1,0:T(8,128)(2,1)} %stiff_hbm.1, bf16[768,768]{1,0:T(8,128)(2,1)} %inverse_hbm.1, bf16[24,768]{1,0:T(8,128)(2,1)} %basis_hbm.1, f32[768]{0:T(1024)} %weights_hbm.1, f32[24,768]{1,0:T(8,128)} %coarse_hbm.1, ...), custom_call_target="tpu_custom_call" | custom-call | tf_op jit(solution)/shard_map/pallas_call | solution.py:355
  19.8 0.6 %slice_bitcast_fusion = (f32[2,768]{1,0:T(2,128)}, f32[2,768]{1,0:T(2,128)}) fusion(f32[2,2,768]{2,1,0:T(2,128)S(1)} %shard_map.122), kind=kLoop, calls=%fused_computation | loop fusion | bytes 24576 | tf_op jit(solution)/shard_map/squeeze | solution.py:386

commit v6 on v5

--- a/solution.py
+++ b/solution.py
@@ -233,21 +233,8 @@
     for step in team_steps:
         share(pl.ds(me, 1), team_mate(step), team_send, team_recv)
 
-    residual_head = own_head - row_mask[:, :head] * exact_dot(arrived, placer[...])
-    residual_bf = jnp.concatenate([residual_head, residual_tail], axis=1).astype(jnp.bfloat16)
-    results[1, :, :head] = residual_head
     got_weights.wait()
     scale = weights[...].reshape(1, order_pad) * row_mask
-    got_inverse.wait()
-    fixed = scale * dot(residual_bf, inverse[...])
-    picked_fix = exact_dot(fixed[:, :head], picker[...])
-    base_out = iterate + fixed
-
-    mates = team * n_sub
-    wait_slabs(mates - 1, team_recv)
-    for step in column_steps:
-        share(pl.ds(team_first * n_sub, mates), column_mate(step), column_send, column_recv)
-
     scaled_basis = scale * basis[...].astype(jnp.float32)
     picked_basis = exact_dot(scaled_basis[:, :head], picker[...])
 
@@ -270,6 +257,19 @@
         return carry
 
     lax.fori_loop(0, devices // group, spread, 0)
+
+    mates = team * n_sub
+    wait_slabs(mates - 1, team_recv)
+    for step in column_steps:
+        share(pl.ds(team_first * n_sub, mates), column_mate(step), column_send, column_recv)
+
+    residual_head = own_head - row_mask[:, :head] * exact_dot(arrived, placer[...])
+    residual_bf = jnp.concatenate([residual_head, residual_tail], axis=1).astype(jnp.bfloat16)
+    results[1, :, :head] = residual_head
+    got_inverse.wait()
+    fixed = scale * dot(residual_bf, inverse[...])
+    picked_fix = exact_dot(fixed[:, :head], picker[...])
+    base_out = iterate + fixed
 
     wait_slabs(devices - mates, column_recv)
 
@@ -330,7 +330,7 @@
 ):
     loads, order_pad = rhs.shape
     directions, slots = out_rows.shape[1:]
-    team = min(t for t in range(1, n_dom + 1) if n_dom % t == 0 and t * t * n_sub >= n_dom)
+    team = max(t for t in range(1, n_dom + 1) if n_dom % t == 0 and (t == 1 or t * t * n_sub <= n_dom))
     vectors = basis.shape[0]
     devices = n_dom * n_sub
     head = -(-(order_pad // 4) // LANES) * LANES

time: 20.6 us -> 20.5 us (level)
  no operation moved by 1% of the time
where the time goes in v6:
time: 20.5 us; the launch traced here: 20.3 us
  Pallas kernels  18.4 us (90%)
  between operations  1.29 us (6%)
  local copies, waits for them, and re-layouts  0.6 us (3%)
    pallas_call x1, Pallas kernels, per_device(): pl.pallas_call(functools.partial(kernel, n_dom, n_sub, team), out_shape=b...  18.4 us
    squeeze x1, local copies, waits for them, and re-layouts, per_device(): return (results[0], results[1])  0.6 us

profile of v6, /device:TPU:0, one launch (start us, length us, event | category | flops | bytes accessed | tf_op | source)
XLA Modules:
  0.0 20.3 jit_solution(1100654434629011523)
XLA Ops:
  1.3 18.4 %shard_map.122 = f32[2,2,768]{2,1,0:T(2,128)S(1)} custom-call(f32[2,768]{1,0:T(2,128)} %rhs_hbm.1, f32[2,768]{1,0:T(2,128)} %start_hbm.1, bf16[768,768]{1,0:T(8,128)(2,1)} %stiff_hbm.1, bf16[768,768]{1,0:T(8,128)(2,1)} %inverse_hbm.1, bf16[24,768]{1,0:T(8,128)(2,1)} %basis_hbm.1, f32[768]{0:T(1024)} %weights_hbm.1, f32[24,768]{1,0:T(8,128)} %coarse_hbm.1, ...), custom_call_target="tpu_custom_call" | custom-call | tf_op jit(solution)/shard_map/pallas_call | solution.py:355
  19.7 0.6 %slice_bitcast_fusion = (f32[2,768]{1,0:T(2,128)}, f32[2,768]{1,0:T(2,128)}) fusion(f32[2,2,768]{2,1,0:T(2,128)S(1)} %shard_map.122), kind=kLoop, calls=%fused_computation | loop fusion | bytes 24576 | tf_op jit(solution)/shard_map/squeeze | solution.py:386
